TPU v7x, 32 devices: a whole 2x2x4 slice. The times are simulated.
32 devices in a mesh: grp: 2 (over y), seq: 4 (over z), chan: 4 (over x, core).
Axes of the slice: x: 2, y: 2, z: 4, core: 2. Of those that a mesh axis runs over, the one named last changes fastest.
Arguments:
- features: bfloat16 [1024, 3, 8192], P(('grp', 'seq'), None, 'chan'), parts along dimension 0, may hold values from -6 to 6
- conv_weight: bfloat16 [7, 3, 8192], P(None, None, 'chan'), may hold values from -2 to 2
- history: bfloat16 [12, 3, 8192], P('grp', None, 'chan'), parts along dimension 0, may hold values from -6 to 6
- pole_rate: float32 [16, 8192], P(None, 'chan'), may hold values from 0.00048828125 to 0.05
- residue: float32 [16, 8192], P(None, 'chan'), may hold values from -6 to 6
- skip_gain: float32 [8192], P('chan'), may hold values from -6 to 6
- start_state: float32 [32, 8192], P('grp', 'chan'), parts along dimension 0, may hold values from -96 to 96
Outputs:
- mixer_out: bfloat16 [1024, 8192], P(('grp', 'seq'), 'chan'), parts along dimension 0
There are 2 independent parts, one for each index of `grp`. A program takes and returns all parts, laid end to end along the dimension named above; an argument that names none is the same for every part. Nothing has to cross between parts.
All inputs are finite; a program needn't handle non-finite values.
Results may differ from a plain program's by a relative error of at most 0.001.
Values may be sent and summed in bfloat16 or wider, within the bound.
A program may use at most 192 MiB of HBM per device.

v0:
```python
import jax
import jax.numpy as jnp
from jax import lax
from jax.sharding import PartitionSpec as P


def passed_along(block, axis, distance):
    devices = range(lax.axis_size(axis))
    route = [(i - distance, i) for i in devices if i - distance in devices]
    return lax.ppermute(block, axis, route)


def carried_in(value, axis, join, neutral):
    count, mine = (lax.axis_size(axis), lax.axis_index(axis))
    pieces = jax.tree.map(lambda part: lax.all_gather(part, axis), value)
    so_far = jax.tree.map(
        lambda part, zero: jnp.full_like(part, 0) + jnp.asarray(zero, part.dtype), value, neutral
    )

    def lap(position, so_far):
        longer = join(so_far, jax.tree.map(lambda part: part[position], pieces))
        return jax.tree.map(lambda new, old: jnp.where(position < mine, new, old), longer, so_far)

    return lax.fori_loop(0, count - 1, lap, so_far)


def body(features, conv_weight, history, pole_rate, residue, skip_gain, start_state):
    length = features.shape[0]
    channels = features.shape[2]
    margin = conv_weight.shape[0] - 1
    preceding = passed_along(features[length - margin :], "seq", 1)
    position = lax.axis_index("seq")
    preceding = jnp.where(position == 0, history, preceding)
    extended = jnp.concatenate([preceding, features], axis=0)
    filtered = jnp.zeros(features.shape, jnp.float32)
    for i in range(margin + 1):
        filtered = filtered + conv_weight[i].astype(jnp.float32) * extended[
            margin - i : margin - i + length
        ].astype(jnp.float32)
    query_part = filtered[:, 0, :]
    product = filtered[:, 1, :] * filtered[:, 2, :]
    pole_gain = residue * jnp.sqrt(2.0 * pole_rate) / 4.0
    block_len = min(64, length)
    block_count = length // block_len
    blocked = product.reshape(block_count, block_len, channels)
    lags = jnp.arange(block_len, dtype=jnp.float32)
    head_decay = jnp.exp(-pole_rate[None] * (lags + 1.0)[:, None, None])
    tail_decay = jnp.exp(-pole_rate[None] * (block_len - 1.0 - lags)[:, None, None])
    kernel_taps = jnp.sum(pole_gain[None] * jnp.exp(-pole_rate[None] * lags[:, None, None]), axis=1)
    offsets = jnp.arange(block_len, dtype=jnp.int32)
    lag_index = offsets[:, None] - offsets[None, :]
    toeplitz = jnp.where((lag_index >= 0)[:, :, None], kernel_taps[jnp.maximum(lag_index, 0)], 0.0)
    block_decay = jnp.exp(-pole_rate * float(block_len))

    def end_state(state, piece):
        added = jnp.einsum("tnc,tc->nc", tail_decay, piece, precision=lax.Precision.HIGHEST)
        return (block_decay * state + added, None)

    stretch_state, unused = lax.scan(end_state, jnp.zeros_like(pole_rate), blocked)
    stretch_span = float(length)

    def combine_count(earlier, later):
        return (
            earlier[0] + later[0],
            jnp.exp(-pole_rate * stretch_span * later[0]) * earlier[1] + later[1],
        )

    counted = carried_in(
        (jnp.ones((1,), jnp.float32), stretch_state),
        "seq",
        combine_count,
        (jnp.zeros((1,), jnp.float32), jnp.zeros_like(stretch_state)),
    )
    entering = jnp.exp(-pole_rate * stretch_span * counted[0]) * start_state + counted[1]

    def block_output(state, piece):
        inner = jnp.einsum("tsc,sc->tc", toeplitz, piece, precision=lax.Precision.HIGHEST)
        carried = jnp.einsum(
            "tnc,nc->tc", head_decay, pole_gain * state, precision=lax.Precision.HIGHEST
        )
        added = jnp.einsum("tnc,tc->nc", tail_decay, piece, precision=lax.Precision.HIGHEST)
        return (block_decay * state + added, inner + carried)

    final_state, convolved = lax.scan(block_output, entering, blocked)
    convolved = convolved.reshape(length, channels)
    return (query_part * (convolved + skip_gain * product)).astype(jnp.bfloat16)


def solution(mesh):
    return jax.shard_map(
        body,
        mesh=mesh,
        in_specs=(
            P(("grp", "seq"), None, "chan"),
            P(None, None, "chan"),
            P("grp", None, "chan"),
            P(None, "chan"),
            P(None, "chan"),
            P("chan"),
            P("grp", "chan"),
        ),
        out_specs=P(("grp", "seq"), "chan"),
        check_vma=False,
    )
```

profile of v0, /device:TPU:0, one launch (start us, length us, event | category | flops | bytes accessed | tf_op | source)
XLA Modules:
  0.0 133.3 jit_solution(4393988778479592161)
XLA Ops:
  0.0 0.9 slice.53
  0.9 4.9 %collective-permute-start = (bf16[6,3,2048]{2,0,1:T(8,128)(2,1)S(1)}, bf16[6,3,2048]{2,0,1:T(8,128)(2,1)S(1)}, u32[]{:S(2)}, u32[]{:S(2)}) collective-permute-start(bf16[6,3,2048]{2,0,1:T(8,128)(2,1)S(1)} %slice.53), channel_id=1, source_target_pairs={{0,4},{4,8},{8,12},{1,5},{5,9},{9,13},{2,6},{6,10},{10,14},{3,7},{... | collective-permute-start | bytes 221192 | tf_op jit(solution)/shard_map/ppermute | solution.py:10
  5.9 1.4 %slice_convert_fusion.6 = (f32[1,3,2048]{2,0,1:T(1,128)S(1)}, f32[1,3,2048]{2,0,1:T(1,128)S(1)}, f32[1,3,2048]{2,0,1:T(1,128)S(1)}, f32[1,3,2048]{2,0,1:T(1,128)...) fusion(bf16[7,3,2048]{2,0,1:T(8,128)(2,1)} %param.14), kind=kLoop, calls=%fused_computation.60 | loop fusion | flops 43008 | bytes 258048 | tf_op jit(solution)/shard_map/mul | solution.py:37
  7.3 1.3 dynamic-slice
  9.3 10.0 %all-reduce = f32[4]{0:T(128)S(1)} all-reduce(f32[4]{0:T(128)S(1)} %dynamic-update-slice), channel_id=1, replica_groups=mesh['grp'=2,'seq'=4,'chan'=4] {'seq'}, use_global_device_ids=true, to_apply=%add | all-reduce | flops 4 | bytes 32
  19.4 1.0 multiply_multiply_fusion
  20.5 2.2 %multiply_reduce_fusion.4 = f32[64,2048]{1,0:T(8,128)S(1)} fusion(f32[16,2048]{1,0:T(8,128)S(1)} %get-tuple-element.631, f32[16,2048]{1,0:T(8,128)S(1)} %get-tuple-element.633), kind=kLoop, calls=%fused_computation.19 | loop fusion | flops 6160384 | bytes 786432 | tf_op jit(solution)/shard_map/reduce_sum | solution.py:49
  22.7 23.8 %gather_fusion = f32[4096,2048]{1,0:T(8,128)} fusion(f32[64,2048]{1,0:T(8,128)S(1)} %multiply_reduce_fusion.4, s32[4096]{0:T(1024)S(1)} %broadcast_clamp_fusion), kind=kCustom, calls=%fused_computation | custom fusion | bytes 67125248 | tf_op jit(solution)/shard_map/gather | solution.py:52
  46.6 23.0 %broadcast_select_fusion = f32[64,64,2048]{2,1,0:T(8,128)} fusion(f32[64,64,2048]{2,1,0:T(8,128)} %bitcast.98, pred[64,64]{1,0:T(8,128)(4,1)S(1)} %subtract_compare_fusion), kind=kLoop, calls=%fused_computation.18 | loop fusion | flops 8388608 | bytes 67112960 | tf_op jit(solution)/shard_map/jit(_where)/select_n | solution.py:52
  69.7 2.9 %multiply_add_fusion = f32[128,3,2048]{2,0,1:T(8,128)S(1)} fusion(bf16[128,3,2048]{2,0,1:T(8,128)(2,1)S(1)} %copy-done.1, bf16[6,3,2048]{2,0,1:T(8,128)(2,1)S(1)} %copy_select_fusion, f32[3,2048]{1,0:T(4,128)S(1)} %get-tuple-element.417, f32[3,2048]{1,0:T(4,128)S(1)} %get-tuple-element.418, f32[3,2048]{1,0:T(4,128)S(1)} %get-tuple-element.419, ...), kind=kLoop, calls=%fused_computation.25 | loop fusion | flops 29884416 | bytes 4964352 | tf_op jit(solution)/shard_map/add | solution.py:37
  72.6 1.6 %copy-done = f32[128,3,2048]{2,0,1:T(8,128)} copy-done((f32[128,3,2048]{2,0,1:T(8,128)}, f32[128,3,2048]{2,0,1:T(8,128)S(1)}, u32[]{:S(2)}) %copy-start) | copy-done | bytes 3145752
  74.4 3.4 %while.43 = (s32[]{:T(128)}, f32[16,2048]{1,0:T(8,128)S(1)}, f32[16,2048]{1,0:T(8,128)S(1)}, f32[2,64,2048]{2,1,0:T(8,128)S(1)}, f32[64]{0:T(128)S(1)}, /*index=5*/f32[16,2048]{1,0:T(8,128)S(1)}, s32[]{:T(128)}, s32[]{:T(128)}) while((s32[]{:T(128)}, f32[16,2048]{1,0:T(8,128)S(1)}, f32[16,2048]{1,0:T(8,128)S(1)}, ...), condition=%wide.region_1.2_spmd.clone, body=%wide.region_0.1_spmd.clone.sunk | while | flops 6356995 | bytes 2359651 | solution.py:59
  74.4 1.6 %multiply_reduce_fusion.9 = f32[2048,16]{0,1:T(8,128)S(1)} fusion(f32[2048,64]{0,1:T(8,128)S(1)} %dynamic-slice_bitcast_fusion.4, f32[64]{0:T(128)S(1)} %get-tuple-element.594, f32[16,2048]{1,0:T(8,128)S(1)} %get-tuple-element.595), kind=kLoop, calls=%fused_computation.7.clone.1 | loop fusion | flops 6258688 | bytes 786688 | tf_op jit(solution)/shard_map/while/body/eval_jaxpr/tnc,tc->nc/dot_general | solution.py:56
  76.1 1.6 %multiply_reduce_fusion.9 = f32[2048,16]{0,1:T(8,128)S(1)} fusion(f32[2048,64]{0,1:T(8,128)S(1)} %dynamic-slice_bitcast_fusion.4, f32[64]{0:T(128)S(1)} %get-tuple-element.594, f32[16,2048]{1,0:T(8,128)S(1)} %get-tuple-element.595), kind=kLoop, calls=%fused_computation.7.clone.1 | loop fusion | flops 6258688 | bytes 786688 | tf_op jit(solution)/shard_map/while/body/eval_jaxpr/tnc,tc->nc/dot_general | solution.py:56
  77.8 14.9 %all-gather = f32[64,2048]{1,0:T(8,128)S(1)} all-gather(f32[16,2048]{1,0:T(8,128)S(1)} %get-tuple-element.250), channel_id=2, replica_groups=mesh['grp'=2,'seq'=4,'chan'=4] {'seq'}, dimensions={0}, use_global_device_ids=true | all-gather | bytes 655360 | tf_op jit(solution)/shard_map/all_gather | solution.py:15
  92.7 5.8 %while.44 = (s32[]{:T(128)}, f32[1]{0:T(128)}, f32[16,2048]{1,0:T(8,128)S(1)}, s32[]{:T(128)}, f32[4,1]{0,1:T(1,128)S(1)}, /*index=5*/f32[16,2048]{1,0:T(8,128)S(1)}, f32[4,16,2048]{2,1,0:T(8,128)S(1)}, s32[]{:T(128)}, s32[]{:T(128)}) while((s32[]{:T(128)}, f32[1]{0:T(128)}, f32[16,2048]{1,0:T(8,128)S(1)}, s32[]{:T(128)}, ...), condition=%wide.region_3.4_spmd.clone, body=%wide.region_2.3_spmd.clone.sunk | while | flops 163847 | bytes 524450 | solution.py:24
  98.6 31.8 %while.45 = (s32[]{:T(128)}, f32[16,2048]{1,0:T(8,128)S(1)}, f32[2,64,2048]{2,1,0:T(8,128)S(1)}, f32[16,2048]{1,0:T(8,128)S(1)}, f32[2,64,2048]{2,1,0:T(8,128)S(...) while((s32[]{:T(128)}, f32[16,2048]{1,0:T(8,128)S(1)}, ...), condition=%wide.region_6.7_spmd.clone.clone, body=%wide.region_5.6_spmd.clone.clone.sunk | while | flops 29294592 | bytes 39584372 | solution.py:84
  98.6 1.6 %multiply_reduce_fusion.10 = f32[2048,16]{0,1:T(8,128)S(1)} fusion(f32[2048,64]{0,1:T(8,128)S(1)} %dynamic-slice_bitcast_fusion.5, f32[64]{0:T(128)S(1)} %get-tuple-element.654, f32[16,2048]{1,0:T(8,128)S(1)} %get-tuple-element.655), kind=kLoop, calls=%fused_computation.13.clone.1 | loop fusion | flops 6258688 | bytes 786688 | tf_op jit(solution)/shard_map/while/body/eval_jaxpr/tnc,tc->nc/dot_general | solution.py:81
  100.3 2.4 %multiply_reduce_fusion.12 = f32[2048,64]{0,1:T(8,128)S(1)} fusion(f32[2048,16]{0,1:T(8,128)S(1)} %get-tuple-element.573, f32[64]{0:T(128)S(1)} %get-tuple-element.656, f32[16,2048]{1,0:T(8,128)S(1)} %get-tuple-element.655), kind=kLoop, calls=%fused_computation.12.clone.1 | loop fusion | flops 6160384 | bytes 786688 | tf_op jit(solution)/shard_map/while/body/eval_jaxpr/tnc,nc->tc/dot_general | solution.py:78
  102.7 11.7 %multiply_reduce_fusion.11 = f32[2048,64]{0,1:T(8,128)S(1)} fusion(f32[64,64,2048]{2,1,0:T(8,128)} %get-tuple-element.652, f32[2048,64]{0,1:T(8,128)S(1)} %dynamic-slice_bitcast_fusion.5), kind=kLoop, calls=%fused_computation.11.clone.1 | loop fusion | flops 16646144 | bytes 34603008 | tf_op jit(solution)/shard_map/while/body/eval_jaxpr/tsc,sc->tc/dot_general | solution.py:77
  114.5 1.6 %multiply_reduce_fusion.10 = f32[2048,16]{0,1:T(8,128)S(1)} fusion(f32[2048,64]{0,1:T(8,128)S(1)} %dynamic-slice_bitcast_fusion.5, f32[64]{0:T(128)S(1)} %get-tuple-element.654, f32[16,2048]{1,0:T(8,128)S(1)} %get-tuple-element.655), kind=kLoop, calls=%fused_computation.13.clone.1 | loop fusion | flops 6258688 | bytes 786688 | tf_op jit(solution)/shard_map/while/body/eval_jaxpr/tnc,tc->nc/dot_general | solution.py:81
  116.2 2.4 %multiply_reduce_fusion.12 = f32[2048,64]{0,1:T(8,128)S(1)} fusion(f32[2048,16]{0,1:T(8,128)S(1)} %get-tuple-element.573, f32[64]{0:T(128)S(1)} %get-tuple-element.656, f32[16,2048]{1,0:T(8,128)S(1)} %get-tuple-element.655), kind=kLoop, calls=%fused_computation.12.clone.1 | loop fusion | flops 6160384 | bytes 786688 | tf_op jit(solution)/shard_map/while/body/eval_jaxpr/tnc,nc->tc/dot_general | solution.py:78
  118.6 11.7 %multiply_reduce_fusion.11 = f32[2048,64]{0,1:T(8,128)S(1)} fusion(f32[64,64,2048]{2,1,0:T(8,128)} %get-tuple-element.652, f32[2048,64]{0,1:T(8,128)S(1)} %dynamic-slice_bitcast_fusion.5), kind=kLoop, calls=%fused_computation.11.clone.1 | loop fusion | flops 16646144 | bytes 34603008 | tf_op jit(solution)/shard_map/while/body/eval_jaxpr/tsc,sc->tc/dot_general | solution.py:77
  130.4 2.9 %fusion.13 = bf16[128,2048]{1,0:T(8,128)(2,1)} fusion(f32[128,3,2048]{2,0,1:T(8,128)} %copy-done, f32[2,64,2048]{2,1,0:T(8,128)S(1)} %get-tuple-element.253, f32[2048]{0:T(1024)S(1)} %copy-done.5), kind=kLoop, calls=%fused_computation.38 | loop fusion | flops 1310720 | bytes 4726784 | tf_op jit(solution)/shard_map/convert_element_type | solution.py:86
  (45 shorter events, 5.6 us)
Async XLA Ops:
  0.9 68.7 %collective-permute-start = (bf16[6,3,2048]{2,0,1:T(8,128)(2,1)S(1)}, bf16[6,3,2048]{2,0,1:T(8,128)(2,1)S(1)}, u32[]{:S(2)}, u32[]{:S(2)}) collective-permute-start(bf16[6,3,2048]{2,0,1:T(8,128)(2,1)S(1)} %slice.53), channel_id=1, source_target_pairs={{0,4},{4,8},{8,12},{1,5},{5,9},{9,13},{2,6},{6,10},{10,14},{3,7},{... | collective-permute-start | bytes 221192 | tf_op jit(solution)/shard_map/ppermute | solution.py:10
  46.6 23.0 %copy-start.4 = (bf16[6,3,2048]{2,1,0:T(4,128)(2,1)S(1)}, bf16[6,3,2048]{2,1,0:T(4,128)(2,1)}, u32[]{:S(2)}) copy-start(bf16[6,3,2048]{2,1,0:T(4,128)(2,1)} %param.15) | copy-start | bytes 221188
  46.6 23.1 %copy-start.1 = (bf16[128,3,2048]{2,0,1:T(8,128)(2,1)S(1)}, bf16[128,3,2048]{2,0,1:T(8,128)(2,1)}, u32[]{:S(2)}) copy-start(bf16[128,3,2048]{2,0,1:T(8,128)(2,1)} %param.13) | copy-start | bytes 4718596
  72.6 1.6 %copy-start = (f32[128,3,2048]{2,0,1:T(8,128)}, f32[128,3,2048]{2,0,1:T(8,128)S(1)}, u32[]{:S(2)}) copy-start(f32[128,3,2048]{2,0,1:T(8,128)S(1)} %multiply_add_fusion) | copy-start | bytes 9437188
  77.8 20.7 %copy-start.2 = (f32[16,2048]{1,0:T(8,128)S(1)}, f32[16,2048]{1,0:T(8,128)}, u32[]{:S(2)}) copy-start(f32[16,2048]{1,0:T(8,128)} %param.16) | copy-start | bytes 393220
  77.8 20.7 %copy-start.3 = (f32[16,2048]{1,0:T(8,128)S(1)}, f32[16,2048]{1,0:T(8,128)}, u32[]{:S(2)}) copy-start(f32[16,2048]{1,0:T(8,128)} %param.19) | copy-start | bytes 393220
  98.6 31.8 %copy-start.5 = (f32[2048]{0:T(1024)S(1)}, f32[2048]{0:T(1024)}, u32[]{:S(2)}) copy-start(f32[2048]{0:T(1024)} %param.18) | copy-start | bytes 24580
where the time goes:
time: 134 us; the launch traced here: 133 us
  other arithmetic  72.5 us (54%)
  local copies, waits for them, and re-layouts  28.7 us (21%)
  blocking collectives  24.8 us (19%)
  starting transfers between devices  4.93 us (4%)
  loops' own time  2.09 us (2%)
    gather x1, local copies, waits for them, and re-layouts, body(): kernel_taps[jnp.maximum(lag_index, 0)]  23.8 us
    dot_general x2, other arithmetic, block_output(): jnp.einsum('tsc,sc->tc', toeplitz, piece, precision=lax.Precision.HIGHEST)  23.4 us
    select_n x1, other arithmetic, body(): jnp.where((lag_index >= 0)[:, :, None], kernel_taps[jnp.maximum(lag_index...  23 us
    all_gather x1, blocking collectives, carried_in(): pieces = jax.tree.map(lambda part: lax.all_gather(part, axis), value)  14.9 us
    unnamed x1, blocking collectives  9.96 us
    ppermute x1, starting transfers between devices, passed_along(): return lax.ppermute(block, axis, route)  4.93 us
    dot_general x2, other arithmetic, block_output(): jnp.einsum('tnc,nc->tc', head_decay, pole_gain * state, precision=lax.Pre...  4.89 us
    unnamed x19, local copies, waits for them, and re-layouts  3.71 us
  transfers between devices with their start and end apart: 1, of which 0 were waited for; matrix products, arithmetic and copies ran while one was open for 40% of the time, Pallas kernels for 0%

commit v1 on v0

v1 whole, which is shorter than its diff:
```python
import functools

import jax
import jax.numpy as jnp
from jax import lax
from jax.experimental import pallas as pl
from jax.experimental.pallas import tpu as pltpu
from jax.sharding import PartitionSpec as P

MESH = pl.DeviceIdType.MESH
SEG = 8
LANES = 128
F32 = jnp.float32


def spread(row):
    return jnp.broadcast_to(row, (SEG, LANES))


def mixer(
    count, per_chunk,
    features, taps, history, rate, residue, skip, start,
    out,
    held, ext, weight, prod, query, inner, decay, seg1, seg2, seg4, whole,
    gain, filt, lift, scanned, send, recv, kv_send, kv_recv, q_send, q_recv, result,
    in_sem, tail_sem, out_sem, state_send, state_recv, halo_send, halo_recv,
):
    parts, tokens, width = held.shape
    margin = taps.shape[1] - 1
    length = tokens // SEG
    columns = width // LANES
    chunks = columns // per_chunk
    span = per_chunk * LANES
    half = width // 2
    poles = rate.shape[0]
    here = lax.axis_index("seq")
    first, last = here == 0, here == count - 1
    onward = lax.rem(here + 1, count)
    back = lax.rem(here + count - 1, count)

    def lanes(c):
        return pl.ds(pl.multiple_of(c * LANES, LANES), LANES)

    def fetch(k):
        area = pl.ds(pl.multiple_of(k * span, span), span)
        return pltpu.make_async_copy(features.at[:, :, area], held.at[:, :, area], in_sem.at[k])

    def put(k):
        area = pl.ds(pl.multiple_of(k * span, span), span)
        return pltpu.make_async_copy(result.at[:, area], out.at[:, area], out_sem.at[k])

    def state_copy(k):
        return pltpu.make_async_remote_copy(
            src_ref=send.at[k], dst_ref=recv.at[k], send_sem=state_send.at[k],
            recv_sem=state_recv.at[k], device_id={"seq": onward}, device_id_type=MESH,
        )

    def halo_copy(src, dst, k):
        return pltpu.make_async_remote_copy(
            src_ref=src, dst_ref=dst, send_sem=halo_send.at[k],
            recv_sem=halo_recv.at[k], device_id={"seq": onward}, device_id_type=MESH,
        )

    kv_copy = halo_copy(kv_send, kv_recv, 0)
    q_copy = halo_copy(q_send, q_recv, 1)

    barrier = pltpu.get_barrier_semaphore()

    @pl.when(jnp.logical_not(first))
    def _():
        pl.semaphore_signal(barrier, inc=1, device_id={"seq": back}, device_id_type=MESH)

    @pl.when(jnp.logical_not(last))
    def _():
        pl.semaphore_signal(barrier, inc=1, device_id={"seq": onward}, device_id_type=MESH)

    for k in range(chunks):
        fetch(k).start()

    rows = lax.broadcasted_iota(jnp.int32, (SEG, LANES), 0)

    def powers(one, two, four):
        value = jnp.where(rows % 2 == 1, one, 1.0)
        value = value * jnp.where((rows // 2) % 2 == 1, two, 1.0)
        return value * jnp.where(rows // 4 == 1, four, 1.0)

    def prepare(c, carry):
        r = rate[:, lanes(c)]
        g = residue[:, lanes(c)] * jnp.sqrt(2.0 * r) / 4.0
        a1 = jnp.exp(-r)
        a2 = jnp.exp(-2.0 * r)
        a4 = jnp.exp(-4.0 * r)
        a8 = jnp.exp(-8.0 * r)
        s1 = jnp.exp(-float(length) * r)
        s2 = jnp.exp(-float(2 * length) * r)
        s4 = jnp.exp(-float(4 * length) * r)
        decay[c] = a1
        gain[c] = g
        seg1[c], seg2[c], seg4[c] = s1, s2, s4
        whole[c] = jnp.exp(-float(tokens) * r)
        block = [jnp.zeros((SEG, LANES), F32) for _ in range(length // SEG)]
        for n in range(poles):
            part = spread(g[n : n + 1]) * powers(
                spread(a1[n : n + 1]), spread(a2[n : n + 1]), spread(a4[n : n + 1])
            )
            up = spread(a8[n : n + 1])
            for b in range(length // SEG):
                block[b] = block[b] + part
                part = part * up
            lift[c, n] = powers(
                spread(s1[n : n + 1]), spread(s2[n : n + 1]), spread(s4[n : n + 1])
            )
        direct = jnp.where(rows == 0, spread(skip[:, lanes(c)]), 0.0)
        block[0] = block[0] + direct
        for b in range(length // SEG):
            filt[c, b * SEG : (b + 1) * SEG] = block[b]
        for j in range(parts):
            weight[c, j * 8 : j * 8 + margin + 1] = taps[j, :, lanes(c)].astype(F32)
        return carry

    for k in range(chunks):
        fetch(k).wait()

    tail = pl.ds(tokens - 16, 16)

    def pack(c, carry):
        k_rows = held[1, tail, lanes(c)].astype(F32)[8:]
        v_rows = held[2, tail, lanes(c)].astype(F32)[8:]
        kv_send[:, lanes(c)] = jnp.concatenate([k_rows, v_rows], axis=0).astype(jnp.bfloat16)
        return carry

    lax.fori_loop(0, columns, pack, 0)

    def pack_q(c, carry):
        low = held[0, tail, lanes(c)].astype(F32)[8:]
        high = held[0, tail, lanes(c + columns // 2)].astype(F32)[8:]
        q_send[:, lanes(c)] = jnp.concatenate([low, high], axis=0).astype(jnp.bfloat16)
        return carry

    lax.fori_loop(0, columns // 2, pack_q, 0)

    peers = jnp.where(first, 0, 1) + jnp.where(last, 0, 1)
    pl.semaphore_wait(barrier, peers)

    @pl.when(jnp.logical_not(last))
    def _():
        kv_copy.start()
        q_copy.start()

    lax.fori_loop(0, columns, prepare, 0)

    def widen(c, carry):
        for j in range(parts):
            ext[j, c, 8 : 8 + tokens] = held[j, :, lanes(c)].astype(F32)
        return carry

    lax.fori_loop(0, columns, widen, 0)

    @pl.when(first)
    def _():
        for i in range(margin):
            row = history[i].astype(F32)
            for j in range(parts):
                for c in range(columns):
                    ext[j, c, 8 - margin + i : 9 - margin + i] = row[
                        j : j + 1, c * LANES : (c + 1) * LANES
                    ]

        def begin(c, carry):
            recv[c // per_chunk, c % per_chunk] = start[:, lanes(c)]
            return carry

        lax.fori_loop(0, columns, begin, 0)

    @pl.when(jnp.logical_not(first))
    def _():
        kv_copy.wait_recv()
        q_copy.wait_recv()

        def unpack(c, carry):
            both = kv_recv[:, lanes(c)].astype(F32)
            ext[1, c, 0:8] = both[:8]
            ext[2, c, 0:8] = both[8:]
            return carry

        lax.fori_loop(0, columns, unpack, 0)

        def unpack_q(c, carry):
            both = q_recv[:, lanes(c)].astype(F32)
            ext[0, c, 0:8] = both[:8]
            ext[0, c + columns // 2, 0:8] = both[8:]
            return carry

        lax.fori_loop(0, columns // 2, unpack_q, 0)

    def filtered(j, c):
        x = [ext[j, c, pl.ds(8 + i, SEG, stride=length), :] for i in range(-margin, length)]
        w = [spread(weight[c, j * 8 + i : j * 8 + i + 1]) for i in range(margin + 1)]
        gained = []
        for t in range(length):
            value = w[0] * x[t + margin]
            for i in range(1, margin + 1):
                value = value + w[i] * x[t + margin - i]
            gained.append(value)
        return gained

    def shifted(value, by):
        return pltpu.roll(value, by, 0)

    def end_states(c, carry):
        left = filtered(1, c)
        right = filtered(2, c)
        p = [u * v for u, v in zip(left, right)]
        for t in range(length):
            prod[c, t] = p[t]
        for n in range(poles):
            a = spread(decay[c, n : n + 1])
            state = p[0]
            for t in range(1, length):
                state = a * state + p[t]
            for by, ref in ((1, seg1), (2, seg2), (4, seg4)):
                step = jnp.where(rows >= by, spread(ref[c, n : n + 1]), 0.0)
                state = state + step * shifted(state, by)
            scanned[c, n * SEG : (n + 1) * SEG] = state
        return carry

    def hand_on(k):
        for m in range(per_chunk):
            c = k * per_chunk + m
            ends = jnp.concatenate(
                [
                    scanned[c, pl.ds(b * 64 + SEG - 1, 8, stride=SEG), :]
                    for b in range(poles // 8)
                ],
                axis=0,
            )
            send[k, m] = whole[c] * recv[k, m] + ends
        state_copy(k).start()

    def first_pass(k, carry):
        lax.fori_loop(k * per_chunk, (k + 1) * per_chunk, end_states, 0)

        @pl.when(jnp.logical_and(first, jnp.logical_not(last)))
        def _():
            hand_on(k)

        return carry

    lax.fori_loop(0, chunks, first_pass, 0)

    def inside(c, carry):
        q = filtered(0, c)
        for t in range(length):
            query[c, t] = q[t]
        p = [prod[c, t] for t in range(length)]
        h = [spread(filt[c, i : i + 1]) for i in range(length)]
        for t in range(length):
            value = h[0] * p[t]
            for i in range(1, t + 1):
                value = value + h[i] * p[t - i]
            inner[c, t] = value
        return carry

    def second_pass(k, carry):
        @pl.when(jnp.logical_and(jnp.logical_not(first), jnp.logical_not(last)))
        def _():
            state_copy(k).wait_recv()
            hand_on(k)

        lax.fori_loop(k * per_chunk, (k + 1) * per_chunk, inside, 0)
        return carry

    lax.fori_loop(0, chunks, second_pass, 0)

    def correct(c, carry):
        k, m = c // per_chunk, c % per_chunk
        w, a = [], []
        for n in range(poles):
            local = jnp.where(rows >= 1, shifted(scanned[c, n * SEG : (n + 1) * SEG], 1), 0.0)
            state = local + lift[c, n] * spread(recv[k, m, n : n + 1])
            w.append(spread(gain[c, n : n + 1]) * state)
            a.append(spread(decay[c, n : n + 1]))
        for t in range(length):
            w = [u * v for u, v in zip(w, a)]
            terms = list(w)
            while len(terms) > 1:
                terms = [terms[i] + terms[i + 1] for i in range(0, len(terms), 2)]
            value = query[c, t] * (inner[c, t] + terms[0])
            ext[0, c, pl.ds(t, SEG, stride=length), :] = value
        result[:, lanes(c)] = ext[0, c, 0:tokens].astype(jnp.bfloat16)
        return carry

    def third_pass(k, carry):
        @pl.when(jnp.logical_and(last, jnp.logical_not(first)))
        def _():
            state_copy(k).wait_recv()

        lax.fori_loop(k * per_chunk, (k + 1) * per_chunk, correct, 0)
        put(k).start()
        return carry

    lax.fori_loop(0, chunks, third_pass, 0)

    @pl.when(jnp.logical_not(last))
    def _():
        kv_copy.wait_send()
        q_copy.wait_send()
        for k in range(chunks):
            state_copy(k).wait_send()

    for k in range(chunks):
        put(k).wait()


def body(features, conv_weight, history, pole_rate, residue, skip_gain, start_state):
    tokens, parts, width = features.shape
    poles = pole_rate.shape[0]
    columns = width // LANES
    per_chunk = 2
    chunks = columns // per_chunk
    length = tokens // SEG
    count = lax.axis_size("seq")
    vmem = pl.BlockSpec(memory_space=pltpu.VMEM)
    hbm = pl.BlockSpec(memory_space=pl.ANY)
    small = pltpu.VMEM((columns, poles, LANES), F32)
    dma = pltpu.SemaphoreType.DMA
    return pl.pallas_call(
        functools.partial(mixer, count, per_chunk),
        out_shape=jax.ShapeDtypeStruct((tokens, width), jnp.bfloat16),
        in_specs=[hbm] + [vmem] * 6,
        out_specs=hbm,
        scratch_shapes=[
            pltpu.VMEM((parts, tokens, width), jnp.bfloat16),
            pltpu.VMEM((parts, columns, tokens + 8, LANES), F32),
            pltpu.VMEM((columns, 8 * parts, LANES), F32),
            pltpu.VMEM((columns, length, SEG, LANES), F32),
            pltpu.VMEM((columns, length, SEG, LANES), F32),
            pltpu.VMEM((columns, length, SEG, LANES), F32),
            small, small, small, small, small, small,
            pltpu.VMEM((columns, length, LANES), F32),
            pltpu.VMEM((columns, poles, SEG, LANES), F32),
            pltpu.VMEM((columns, poles * SEG, LANES), F32),
            pltpu.VMEM((chunks, per_chunk, poles, LANES), F32),
            pltpu.VMEM((chunks, per_chunk, poles, LANES), F32),
            pltpu.VMEM((16, width), jnp.bfloat16),
            pltpu.VMEM((16, width), jnp.bfloat16),
            pltpu.VMEM((16, width // 2), jnp.bfloat16),
            pltpu.VMEM((16, width // 2), jnp.bfloat16),
            pltpu.VMEM((tokens, width), jnp.bfloat16),
            dma((chunks,)), dma((1,)), dma((chunks,)), dma((chunks,)), dma((chunks,)),
            dma((2,)), dma((2,)),
        ],
        compiler_params=pltpu.CompilerParams(
            collective_id=0, has_side_effects=True, vmem_limit_bytes=40 * 1024 * 1024
        ),
    )(
        features.transpose(1, 0, 2), conv_weight.transpose(1, 0, 2), history,
        pole_rate, residue, skip_gain[None], start_state,
    )


def solution(mesh):
    return jax.shard_map(
        body,
        mesh=mesh,
        in_specs=(
            P(("grp", "seq"), None, "chan"),
            P(None, None, "chan"),
            P("grp", None, "chan"),
            P(None, "chan"),
            P(None, "chan"),
            P("chan"),
            P("grp", "chan"),
        ),
        out_specs=P(("grp", "seq"), "chan"),
        check_vma=False,
    )
```

time: 134 us -> 22 us (0.16)
  the two profiles are of different devices: /device:TPU:0 before, /device:TPU:26 now
where the time goes in v1:
time: 22 us; the launch traced here: 21.7 us
  Pallas kernels  14.3 us (65%)
  local copies, waits for them, and re-layouts  7.39 us (34%)
    pallas_call x1, Pallas kernels, body(): pl.pallas_call(functools.partial(mixer, count, per_chunk), out_shape=jax....  14.3 us
    unnamed x15, local copies, waits for them, and re-layouts  7.39 us

profile of v1, /device:TPU:26, one launch (start us, length us, event | category | flops | bytes accessed | tf_op | source)
XLA Modules:
  0.0 21.7 jit_solution(9914660189897268707)
XLA Ops:
  0.0 0.0 copy-start
  0.0 1.4 %copy-done = bf16[128,3,2048]{2,0,1:T(8,128)(2,1)S(1)} copy-done((bf16[128,3,2048]{2,0,1:T(8,128)(2,1)S(1)}, bf16[128,3,2048]{2,0,1:T(8,128)(2,1)}, u32[]{:S(2)}) %copy-start) | copy-done | bytes 1572888
  1.4 0.0 copy-start.1
  1.4 0.9 %copy-done.1 = f32[16,2048]{1,0:T(8,128)S(1)} copy-done((f32[16,2048]{1,0:T(8,128)S(1)}, f32[16,2048]{1,0:T(8,128)}, u32[]{:S(2)}) %copy-start.1) | copy-done | bytes 131096
  2.3 0.0 copy-start.2
  2.3 0.9 %copy-done.2 = f32[16,2048]{1,0:T(8,128)S(1)} copy-done((f32[16,2048]{1,0:T(8,128)S(1)}, f32[16,2048]{1,0:T(8,128)}, u32[]{:S(2)}) %copy-start.2) | copy-done | bytes 131096
  3.2 0.0 copy-start.3
  3.2 0.9 %copy-done.3 = f32[16,2048]{1,0:T(8,128)S(1)} copy-done((f32[16,2048]{1,0:T(8,128)S(1)}, f32[16,2048]{1,0:T(8,128)}, u32[]{:S(2)}) %copy-start.3) | copy-done | bytes 131096
  4.1 0.0 copy-start.4
  4.1 0.9 %copy-done.4 = bf16[7,3,2048]{2,0,1:T(8,128)(2,1)S(1)} copy-done((bf16[7,3,2048]{2,0,1:T(8,128)(2,1)S(1)}, bf16[7,3,2048]{2,0,1:T(8,128)(2,1)}, u32[]{:S(2)}) %copy-start.4) | copy-done | bytes 86040
  5.0 0.0 copy-start.5
  5.0 0.9 %copy-done.5 = bf16[6,3,2048]{2,1,0:T(4,128)(2,1)S(1)} copy-done((bf16[6,3,2048]{2,1,0:T(4,128)(2,1)S(1)}, bf16[6,3,2048]{2,1,0:T(4,128)(2,1)}, u32[]{:S(2)}) %copy-start.5) | copy-done | bytes 73752
  5.9 0.0 copy-start.6
  5.9 0.7 %copy-done.6 = f32[2048]{0:T(1024)S(1)} copy-done((f32[2048]{0:T(1024)S(1)}, f32[2048]{0:T(1024)}, u32[]{:S(2)}) %copy-start.6) | copy-done | bytes 8216
  6.6 14.3 %shard_map.73 = bf16[128,2048]{1,0:T(8,128)(2,1)S(1)} custom-call(bf16[3,128,2048]{2,1,0:T(8,128)(2,1)S(1)} %bitcast.3, bf16[3,7,2048]{2,1,0:T(8,128)(2,1)S(1)} %bitcast.4, bf16[6,3,2048]{2,1,0:T(4,128)(2,1)S(1)} %copy-done.5, f32[16,2048]{1,0:T(8,128)S(1)} %copy-done.1, f32[16,2048]{1,0:T(8,128)S(1)} %copy-done.2, f32[1,2048]{1,0:T(1,128)S(1)} %bitcast.5, ...), custom_call_target="tpu_custom_call" | custom-call | tf_op jit(solution)/shard_map/pallas_call | solution.py:327
  20.9 0.8 %copy.9 = bf16[128,2048]{1,0:T(8,128)(2,1)} copy(bf16[128,2048]{1,0:T(8,128)(2,1)S(1)} %shard_map.73) | data formatting | bytes 1048576
Async XLA Ops:
  0.0 1.4 %copy-start = (bf16[128,3,2048]{2,0,1:T(8,128)(2,1)S(1)}, bf16[128,3,2048]{2,0,1:T(8,128)(2,1)}, u32[]{:S(2)}) copy-start(bf16[128,3,2048]{2,0,1:T(8,128)(2,1)} %param.7) | copy-start | bytes 4718596
  1.4 0.9 %copy-start.1 = (f32[16,2048]{1,0:T(8,128)S(1)}, f32[16,2048]{1,0:T(8,128)}, u32[]{:S(2)}) copy-start(f32[16,2048]{1,0:T(8,128)} %rate.1) | copy-start | bytes 393220
  2.3 0.9 %copy-start.2 = (f32[16,2048]{1,0:T(8,128)S(1)}, f32[16,2048]{1,0:T(8,128)}, u32[]{:S(2)}) copy-start(f32[16,2048]{1,0:T(8,128)} %residue.1) | copy-start | bytes 393220
  3.2 0.9 %copy-start.3 = (f32[16,2048]{1,0:T(8,128)S(1)}, f32[16,2048]{1,0:T(8,128)}, u32[]{:S(2)}) copy-start(f32[16,2048]{1,0:T(8,128)} %start.1) | copy-start | bytes 393220
  4.1 0.9 %copy-start.4 = (bf16[7,3,2048]{2,0,1:T(8,128)(2,1)S(1)}, bf16[7,3,2048]{2,0,1:T(8,128)(2,1)}, u32[]{:S(2)}) copy-start(bf16[7,3,2048]{2,0,1:T(8,128)(2,1)} %param.8) | copy-start | bytes 258052
  5.0 0.9 %copy-start.5 = (bf16[6,3,2048]{2,1,0:T(4,128)(2,1)S(1)}, bf16[6,3,2048]{2,1,0:T(4,128)(2,1)}, u32[]{:S(2)}) copy-start(bf16[6,3,2048]{2,1,0:T(4,128)(2,1)} %history.1) | copy-start | bytes 221188
  5.9 0.7 %copy-start.6 = (f32[2048]{0:T(1024)S(1)}, f32[2048]{0:T(1024)}, u32[]{:S(2)}) copy-start(f32[2048]{0:T(1024)} %param.12) | copy-start | bytes 24580

commit v2 on v1

--- a/solution.py
+++ b/solution.py
@@ -19,11 +19,11 @@
 
 def mixer(
     count, per_chunk,
-    features, taps, history, rate, residue, skip, start,
+    features, taps_in, history_in, rate_in, residue_in, skip_in, start_in,
     out,
-    held, ext, weight, prod, query, inner, decay, seg1, seg2, seg4, whole,
+    taps, history, rate, residue, skip, start, ends_here, held, ext, weight, prod, query, inner, decay, seg1, seg2, seg4, whole,
     gain, filt, lift, scanned, send, recv, kv_send, kv_recv, q_send, q_recv, result,
-    in_sem, tail_sem, out_sem, state_send, state_recv, halo_send, halo_recv,
+    in_sem, own_sem, out_sem, state_send, state_recv, halo_send, halo_recv,
 ):
     parts, tokens, width = held.shape
     margin = taps.shape[1] - 1
@@ -74,6 +74,23 @@
     def _():
         pl.semaphore_signal(barrier, inc=1, device_id={"seq": onward}, device_id_type=MESH)
 
+    tail = pl.ds(tokens - 16, 16)
+    owned = [
+        pltpu.make_async_copy(src, dst, own_sem.at[i])
+        for i, (src, dst) in enumerate(
+            (
+                (features.at[:, tail], ends_here),
+                (rate_in, rate),
+                (residue_in, residue),
+                (skip_in, skip),
+                (taps_in, taps),
+                (start_in, start),
+                (history_in, history),
+            )
+        )
+    ]
+    for copy in owned:
+        copy.start()
     for k in range(chunks):
         fetch(k).start()
 
@@ -118,22 +135,19 @@
             weight[c, j * 8 : j * 8 + margin + 1] = taps[j, :, lanes(c)].astype(F32)
         return carry
 
-    for k in range(chunks):
-        fetch(k).wait()
-
-    tail = pl.ds(tokens - 16, 16)
+    owned[0].wait()
 
     def pack(c, carry):
-        k_rows = held[1, tail, lanes(c)].astype(F32)[8:]
-        v_rows = held[2, tail, lanes(c)].astype(F32)[8:]
+        k_rows = ends_here[1, :, lanes(c)].astype(F32)[8:]
+        v_rows = ends_here[2, :, lanes(c)].astype(F32)[8:]
         kv_send[:, lanes(c)] = jnp.concatenate([k_rows, v_rows], axis=0).astype(jnp.bfloat16)
         return carry
 
     lax.fori_loop(0, columns, pack, 0)
 
     def pack_q(c, carry):
-        low = held[0, tail, lanes(c)].astype(F32)[8:]
-        high = held[0, tail, lanes(c + columns // 2)].astype(F32)[8:]
+        low = ends_here[0, :, lanes(c)].astype(F32)[8:]
+        high = ends_here[0, :, lanes(c + columns // 2)].astype(F32)[8:]
         q_send[:, lanes(c)] = jnp.concatenate([low, high], axis=0).astype(jnp.bfloat16)
         return carry
 
@@ -147,6 +161,8 @@
         kv_copy.start()
         q_copy.start()
 
+    for copy in owned[1:]:
+        copy.wait()
     lax.fori_loop(0, columns, prepare, 0)
 
     def widen(c, carry):
@@ -154,7 +170,12 @@
             ext[j, c, 8 : 8 + tokens] = held[j, :, lanes(c)].astype(F32)
         return carry
 
-    lax.fori_loop(0, columns, widen, 0)
+    def widen_chunk(k, carry):
+        fetch(k).wait()
+        lax.fori_loop(k * per_chunk, (k + 1) * per_chunk, widen, 0)
+        return carry
+
+    lax.fori_loop(0, chunks, widen_chunk, 0)
 
     @pl.when(first)
     def _():
@@ -244,6 +265,11 @@
         def _():
             hand_on(k)
 
+        @pl.when(jnp.logical_and(here == 1, jnp.logical_not(last)))
+        def _():
+            state_copy(k).wait_recv()
+            hand_on(k)
+
         return carry
 
     lax.fori_loop(0, chunks, first_pass, 0)
@@ -262,7 +288,7 @@
         return carry
 
     def second_pass(k, carry):
-        @pl.when(jnp.logical_and(jnp.logical_not(first), jnp.logical_not(last)))
+        @pl.when(jnp.logical_and(here > 1, jnp.logical_not(last)))
         def _():
             state_copy(k).wait_recv()
             hand_on(k)
@@ -320,16 +346,22 @@
     chunks = columns // per_chunk
     length = tokens // SEG
     count = lax.axis_size("seq")
-    vmem = pl.BlockSpec(memory_space=pltpu.VMEM)
-    hbm = pl.BlockSpec(memory_space=pl.ANY)
+    hbm = pl.BlockSpec(memory_space=pltpu.HBM)
     small = pltpu.VMEM((columns, poles, LANES), F32)
     dma = pltpu.SemaphoreType.DMA
     return pl.pallas_call(
         functools.partial(mixer, count, per_chunk),
         out_shape=jax.ShapeDtypeStruct((tokens, width), jnp.bfloat16),
-        in_specs=[hbm] + [vmem] * 6,
+        in_specs=[hbm] * 7,
         out_specs=hbm,
         scratch_shapes=[
+            pltpu.VMEM((parts,) + conv_weight.shape[:1] + (width,), jnp.bfloat16),
+            pltpu.VMEM(history.shape, jnp.bfloat16),
+            pltpu.VMEM((poles, width), F32),
+            pltpu.VMEM((poles, width), F32),
+            pltpu.VMEM((1, width), F32),
+            pltpu.VMEM((poles, width), F32),
+            pltpu.VMEM((parts, 16, width), jnp.bfloat16),
             pltpu.VMEM((parts, tokens, width), jnp.bfloat16),
             pltpu.VMEM((parts, columns, tokens + 8, LANES), F32),
             pltpu.VMEM((columns, 8 * parts, LANES), F32),
@@ -347,11 +379,11 @@
             pltpu.VMEM((16, width // 2), jnp.bfloat16),
             pltpu.VMEM((16, width // 2), jnp.bfloat16),
             pltpu.VMEM((tokens, width), jnp.bfloat16),
-            dma((chunks,)), dma((1,)), dma((chunks,)), dma((chunks,)), dma((chunks,)),
+            dma((chunks,)), dma((7,)), dma((chunks,)), dma((chunks,)), dma((chunks,)),
             dma((2,)), dma((2,)),
         ],
         compiler_params=pltpu.CompilerParams(
-            collective_id=0, has_side_effects=True, vmem_limit_bytes=40 * 1024 * 1024
+            collective_id=0, has_side_effects=True, vmem_limit_bytes=60 * 1024 * 1024
         ),
     )(
         features.transpose(1, 0, 2), conv_weight.transpose(1, 0, 2), history,

time: 22 us -> 16.7 us (0.76)
  local copies, waits for them, and re-layouts: 7.39 us -> 1.88 us
  Pallas kernels: 14.3 us -> 14.6 us
    unnamed x15 -> x1, local copies, waits for them, and re-layouts: 7.39 us -> 1.88 us
    pallas_call x1, Pallas kernels: 14.3 us -> 14.6 us  [body(): pl.pallas_call(functools.partial(mixer, count, per_chunk), out_shape=jax....]
where the time goes in v2:
time: 16.7 us; the launch traced here: 16.5 us
  Pallas kernels  14.6 us (87%)
  local copies, waits for them, and re-layouts  1.88 us (11%)
    pallas_call x1, Pallas kernels, body(): pl.pallas_call(functools.partial(mixer, count, per_chunk), out_shape=jax....  14.6 us
    unnamed x1, local copies, waits for them, and re-layouts  1.88 us

profile of v2, /device:TPU:26, one launch (start us, length us, event | category | flops | bytes accessed | tf_op | source)
XLA Modules:
  0.0 16.5 jit_solution(508580443788562217)
XLA Ops:
  0.0 14.6 %shard_map.73 = bf16[128,2048]{1,0:T(8,128)(2,1)} custom-call(bf16[3,128,2048]{2,1,0:T(8,128)(2,1)} %bitcast.3, bf16[3,7,2048]{2,1,0:T(8,128)(2,1)} %bitcast.4, bf16[6,3,2048]{2,1,0:T(4,128)(2,1)} %history_in.1, f32[16,2048]{1,0:T(8,128)} %rate_in.1, f32[16,2048]{1,0:T(8,128)} %residue_in.1, f32[1,2048]{1,0:T(1,128)} %bitcast.5, f32[16,2048]{1,0:T(8,128)} %start_in.1), custom_call_target="tpu_custom_call" | custom-call | tf_op jit(solution)/shard_map/pallas_call | solution.py:352
  14.6 1.9 %copy.9 = bf16[128,2048]{1,0:T(8,128)(2,1)} copy(bf16[128,2048]{1,0:T(8,128)(2,1)} %shard_map.73) | data formatting | bytes 1048576

commit v3 on v2

--- a/solution.py
+++ b/solution.py
@@ -21,7 +21,7 @@
     count, per_chunk,
     features, taps_in, history_in, rate_in, residue_in, skip_in, start_in,
     out,
-    taps, history, rate, residue, skip, start, ends_here, held, ext, weight, prod, query, inner, decay, seg1, seg2, seg4, whole,
+    taps, history, rate, residue, skip, start, ends_here, held, ext, weight, prod, query, inner, decay, rest, seg1, seg2, seg4, whole,
     gain, filt, lift, scanned, send, recv, kv_send, kv_recv, q_send, q_recv, result,
     in_sem, own_sem, out_sem, state_send, state_recv, halo_send, halo_recv,
 ):
@@ -103,18 +103,25 @@
 
     def prepare(c, carry):
         r = rate[:, lanes(c)]
+        decay[c] = jnp.exp(-r)
+        rest[c] = jnp.exp(-float(length - margin) * r)
+        seg1[c] = jnp.exp(-float(length) * r)
+        seg2[c] = jnp.exp(-float(2 * length) * r)
+        seg4[c] = jnp.exp(-float(4 * length) * r)
+        whole[c] = jnp.exp(-float(tokens) * r)
+        for j in range(parts):
+            weight[c, j * 8 : j * 8 + margin + 1] = taps[j, :, lanes(c)].astype(F32)
+        return carry
+
+    def prepare_more(c, carry):
+        r = rate[:, lanes(c)]
         g = residue[:, lanes(c)] * jnp.sqrt(2.0 * r) / 4.0
-        a1 = jnp.exp(-r)
+        a1 = decay[c]
         a2 = jnp.exp(-2.0 * r)
         a4 = jnp.exp(-4.0 * r)
         a8 = jnp.exp(-8.0 * r)
-        s1 = jnp.exp(-float(length) * r)
-        s2 = jnp.exp(-float(2 * length) * r)
-        s4 = jnp.exp(-float(4 * length) * r)
-        decay[c] = a1
+        s1, s2, s4 = seg1[c], seg2[c], seg4[c]
         gain[c] = g
-        seg1[c], seg2[c], seg4[c] = s1, s2, s4
-        whole[c] = jnp.exp(-float(tokens) * r)
         block = [jnp.zeros((SEG, LANES), F32) for _ in range(length // SEG)]
         for n in range(poles):
             part = spread(g[n : n + 1]) * powers(
@@ -131,8 +138,6 @@
         block[0] = block[0] + direct
         for b in range(length // SEG):
             filt[c, b * SEG : (b + 1) * SEG] = block[b]
-        for j in range(parts):
-            weight[c, j * 8 : j * 8 + margin + 1] = taps[j, :, lanes(c)].astype(F32)
         return carry
 
     owned[0].wait()
@@ -161,88 +166,56 @@
         kv_copy.start()
         q_copy.start()
 
-    for copy in owned[1:]:
-        copy.wait()
-    lax.fori_loop(0, columns, prepare, 0)
-
-    def widen(c, carry):
-        for j in range(parts):
-            ext[j, c, 8 : 8 + tokens] = held[j, :, lanes(c)].astype(F32)
-        return carry
-
-    def widen_chunk(k, carry):
-        fetch(k).wait()
-        lax.fori_loop(k * per_chunk, (k + 1) * per_chunk, widen, 0)
-        return carry
-
-    lax.fori_loop(0, chunks, widen_chunk, 0)
-
-    @pl.when(first)
-    def _():
-        for i in range(margin):
-            row = history[i].astype(F32)
-            for j in range(parts):
-                for c in range(columns):
-                    ext[j, c, 8 - margin + i : 9 - margin + i] = row[
-                        j : j + 1, c * LANES : (c + 1) * LANES
-                    ]
-
-        def begin(c, carry):
-            recv[c // per_chunk, c % per_chunk] = start[:, lanes(c)]
-            return carry
-
-        lax.fori_loop(0, columns, begin, 0)
-
-    @pl.when(jnp.logical_not(first))
-    def _():
-        kv_copy.wait_recv()
-        q_copy.wait_recv()
-
-        def unpack(c, carry):
-            both = kv_recv[:, lanes(c)].astype(F32)
-            ext[1, c, 0:8] = both[:8]
-            ext[2, c, 0:8] = both[8:]
-            return carry
-
-        lax.fori_loop(0, columns, unpack, 0)
-
-        def unpack_q(c, carry):
-            both = q_recv[:, lanes(c)].astype(F32)
-            ext[0, c, 0:8] = both[:8]
-            ext[0, c + columns // 2, 0:8] = both[8:]
-            return carry
-
-        lax.fori_loop(0, columns // 2, unpack_q, 0)
-
-    def filtered(j, c):
-        x = [ext[j, c, pl.ds(8 + i, SEG, stride=length), :] for i in range(-margin, length)]
+    def filtered(j, c, low, high):
+        x = [ext[j, c, pl.ds(8 + i, SEG, stride=length), :] for i in range(low - margin, high)]
         w = [spread(weight[c, j * 8 + i : j * 8 + i + 1]) for i in range(margin + 1)]
         gained = []
-        for t in range(length):
+        for t in range(high - low):
             value = w[0] * x[t + margin]
             for i in range(1, margin + 1):
                 value = value + w[i] * x[t + margin - i]
             gained.append(value)
         return gained
 
+    def product(c, low, high):
+        p = [u * v for u, v in zip(filtered(1, c, low, high), filtered(2, c, low, high))]
+        for t in range(low, high):
+            prod[c, t] = p[t - low]
+        return p
+
+    def summed(c, n, p):
+        a = spread(decay[c, n : n + 1])
+        state = p[0]
+        for value in p[1:]:
+            state = a * state + value
+        return state
+
     def shifted(value, by):
         return pltpu.roll(value, by, 0)
 
+    def scan_segments(c, n, state):
+        for by, ref in ((1, seg1), (2, seg2), (4, seg4)):
+            step = jnp.where(rows >= by, spread(ref[c, n : n + 1]), 0.0)
+            state = state + step * shifted(state, by)
+        scanned[c, n * SEG : (n + 1) * SEG] = state
+
     def end_states(c, carry):
-        left = filtered(1, c)
-        right = filtered(2, c)
-        p = [u * v for u, v in zip(left, right)]
-        for t in range(length):
-            prod[c, t] = p[t]
+        p = product(c, 0, length)
         for n in range(poles):
-            a = spread(decay[c, n : n + 1])
-            state = p[0]
-            for t in range(1, length):
-                state = a * state + p[t]
-            for by, ref in ((1, seg1), (2, seg2), (4, seg4)):
-                step = jnp.where(rows >= by, spread(ref[c, n : n + 1]), 0.0)
-                state = state + step * shifted(state, by)
-            scanned[c, n * SEG : (n + 1) * SEG] = state
+            scan_segments(c, n, summed(c, n, p))
+        return carry
+
+    def end_states_early(c, carry):
+        p = product(c, margin, length)
+        for n in range(poles):
+            scanned[c, n * SEG : (n + 1) * SEG] = summed(c, n, p)
+        return carry
+
+    def end_states_late(c, carry):
+        p = product(c, 0, margin)
+        for n in range(poles):
+            early = scanned[c, n * SEG : (n + 1) * SEG]
+            scan_segments(c, n, early + spread(rest[c, n : n + 1]) * summed(c, n, p))
         return carry
 
     def hand_on(k):
@@ -258,24 +231,89 @@
             send[k, m] = whole[c] * recv[k, m] + ends
         state_copy(k).start()
 
-    def first_pass(k, carry):
-        lax.fori_loop(k * per_chunk, (k + 1) * per_chunk, end_states, 0)
-
-        @pl.when(jnp.logical_and(first, jnp.logical_not(last)))
-        def _():
-            hand_on(k)
-
-        @pl.when(jnp.logical_and(here == 1, jnp.logical_not(last)))
-        def _():
-            state_copy(k).wait_recv()
-            hand_on(k)
-
-        return carry
-
-    lax.fori_loop(0, chunks, first_pass, 0)
+    for copy in owned[1:]:
+        copy.wait()
+    lax.fori_loop(0, columns, prepare, 0)
+
+    def widen(c, carry):
+        for j in range(parts):
+            ext[j, c, 8 : 8 + tokens] = held[j, :, lanes(c)].astype(F32)
+        return carry
+
+    def each(k, step):
+        lax.fori_loop(k * per_chunk, (k + 1) * per_chunk, step, 0)
+
+    @pl.when(first)
+    def _():
+        for i in range(margin):
+            row = history[i].astype(F32)
+            for j in range(parts):
+                for c in range(columns):
+                    ext[j, c, 8 - margin + i : 9 - margin + i] = row[
+                        j : j + 1, c * LANES : (c + 1) * LANES
+                    ]
+
+        def begin(c, carry):
+            recv[c // per_chunk, c % per_chunk] = start[:, lanes(c)]
+            return carry
+
+        lax.fori_loop(0, columns, begin, 0)
+
+        def only_pass(k, carry):
+            fetch(k).wait()
+            each(k, widen)
+            each(k, end_states)
+
+            @pl.when(jnp.logical_not(last))
+            def _():
+                hand_on(k)
+
+            return carry
+
+        lax.fori_loop(0, chunks, only_pass, 0)
+
+    @pl.when(jnp.logical_not(first))
+    def _():
+        def early_pass(k, carry):
+            fetch(k).wait()
+            each(k, widen)
+            each(k, end_states_early)
+            return carry
+
+        lax.fori_loop(0, chunks, early_pass, 0)
+        kv_copy.wait_recv()
+        q_copy.wait_recv()
+
+        def unpack(c, carry):
+            both = kv_recv[:, lanes(c)].astype(F32)
+            ext[1, c, 0:8] = both[:8]
+            ext[2, c, 0:8] = both[8:]
+            return carry
+
+        lax.fori_loop(0, columns, unpack, 0)
+
+        def unpack_q(c, carry):
+            both = q_recv[:, lanes(c)].astype(F32)
+            ext[0, c, 0:8] = both[:8]
+            ext[0, c + columns // 2, 0:8] = both[8:]
+            return carry
+
+        lax.fori_loop(0, columns // 2, unpack_q, 0)
+
+        def late_pass(k, carry):
+            each(k, end_states_late)
+
+            @pl.when(jnp.logical_and(here == 1, jnp.logical_not(last)))
+            def _():
+                state_copy(k).wait_recv()
+                hand_on(k)
+
+            return carry
+
+        lax.fori_loop(0, chunks, late_pass, 0)
 
     def inside(c, carry):
-        q = filtered(0, c)
+        q = filtered(0, c, 0, length)
         for t in range(length):
             query[c, t] = q[t]
         p = [prod[c, t] for t in range(length)]
@@ -293,7 +331,8 @@
             state_copy(k).wait_recv()
             hand_on(k)
 
-        lax.fori_loop(k * per_chunk, (k + 1) * per_chunk, inside, 0)
+        each(k, prepare_more)
+        each(k, inside)
         return carry
 
     lax.fori_loop(0, chunks, second_pass, 0)
@@ -321,7 +360,7 @@
         def _():
             state_copy(k).wait_recv()
 
-        lax.fori_loop(k * per_chunk, (k + 1) * per_chunk, correct, 0)
+        each(k, correct)
         put(k).start()
         return carry
 
@@ -336,6 +375,20 @@
 
     for k in range(chunks):
         put(k).wait()
+
+
+def settle(parts, source, out, sem):
+    rows = source.shape[0] // parts
+    copies = [
+        pltpu.make_async_copy(
+            source.at[pl.ds(i * rows, rows)], out.at[pl.ds(i * rows, rows)], sem.at[i]
+        )
+        for i in range(parts)
+    ]
+    for copy in copies:
+        copy.start()
+    for copy in copies:
+        copy.wait()
 
 
 def body(features, conv_weight, history, pole_rate, residue, skip_gain, start_state):
@@ -349,7 +402,7 @@
     hbm = pl.BlockSpec(memory_space=pltpu.HBM)
     small = pltpu.VMEM((columns, poles, LANES), F32)
     dma = pltpu.SemaphoreType.DMA
-    return pl.pallas_call(
+    mixed = pl.pallas_call(
         functools.partial(mixer, count, per_chunk),
         out_shape=jax.ShapeDtypeStruct((tokens, width), jnp.bfloat16),
         in_specs=[hbm] * 7,
@@ -368,7 +421,7 @@
             pltpu.VMEM((columns, length, SEG, LANES), F32),
             pltpu.VMEM((columns, length, SEG, LANES), F32),
             pltpu.VMEM((columns, length, SEG, LANES), F32),
-            small, small, small, small, small, small,
+            small, small, small, small, small, small, small,
             pltpu.VMEM((columns, length, LANES), F32),
             pltpu.VMEM((columns, poles, SEG, LANES), F32),
             pltpu.VMEM((columns, poles * SEG, LANES), F32),
@@ -389,6 +442,14 @@
         features.transpose(1, 0, 2), conv_weight.transpose(1, 0, 2), history,
         pole_rate, residue, skip_gain[None], start_state,
     )
+    pieces = tokens // 16
+    return pl.pallas_call(
+        functools.partial(settle, pieces),
+        out_shape=jax.ShapeDtypeStruct((tokens, width), jnp.bfloat16),
+        in_specs=[hbm],
+        out_specs=hbm,
+        scratch_shapes=[dma((pieces,))],
+    )(mixed)
 
 
 def solution(mesh):

time: 16.7 us -> 30.7 us (1.84)
  Pallas kernels: 14.6 us -> 30.6 us
  local copies, waits for them, and re-layouts: 1.88 us -> 0 us
    pallas_call x0 -> x1, Pallas kernels: none -> 17.1 us  [body(): pl.pallas_call(functools.partial(settle, pieces), out_shape=jax.ShapeDtyp...]
    unnamed x1 -> x0, local copies, waits for them, and re-layouts: 1.88 us -> none
    pallas_call x1, Pallas kernels: 14.6 us -> 13.5 us  [body(): pl.pallas_call(functools.partial(mixer, count, per_chunk), out_shape=jax....]
where the time goes in v3:
time: 30.7 us; the launch traced here: 30.6 us
  Pallas kernels  30.6 us (100%)
    pallas_call x1, Pallas kernels, body(): pl.pallas_call(functools.partial(settle, pieces), out_shape=jax.ShapeDtyp...  17.1 us
    pallas_call x1, Pallas kernels, body(): pl.pallas_call(functools.partial(mixer, count, per_chunk), out_shape=jax....  13.5 us

profile of v3, /device:TPU:26, one launch (start us, length us, event | category | flops | bytes accessed | tf_op | source)
XLA Modules:
  0.0 30.6 jit_solution(3850611056493533961)
XLA Ops:
  0.0 13.5 %shard_map.73.source = bf16[128,2048]{1,0:T(8,128)(2,1)} custom-call(bf16[3,128,2048]{2,1,0:T(8,128)(2,1)} %bitcast.3, bf16[3,7,2048]{2,1,0:T(8,128)(2,1)} %bitcast.4, bf16[6,3,2048]{2,1,0:T(4,128)(2,1)} %history_in.1, f32[16,2048]{1,0:T(8,128)} %rate_in.1, f32[16,2048]{1,0:T(8,128)} %residue_in.1, f32[1,2048]{1,0:T(1,128)} %bitcast.5, f32[16,2048]{1,0:T(8,128)} %start_in.1), custom_call_target="tpu_custom_call" | custom-call | tf_op jit(solution)/shard_map/pallas_call | solution.py:405
  13.5 17.1 %shard_map.74 = bf16[128,2048]{1,0:T(8,128)(2,1)} custom-call(bf16[128,2048]{1,0:T(8,128)(2,1)} %shard_map.73.source), custom_call_target="tpu_custom_call" | custom-call | tf_op jit(solution)/shard_map/pallas_call | solution.py:446

commit v4 on v3

--- a/solution.py
+++ b/solution.py
@@ -22,8 +22,8 @@
     features, taps_in, history_in, rate_in, residue_in, skip_in, start_in,
     out,
     taps, history, rate, residue, skip, start, ends_here, held, ext, weight, prod, query, inner, decay, rest, seg1, seg2, seg4, whole,
-    gain, filt, lift, scanned, send, recv, kv_send, kv_recv, q_send, q_recv, result,
-    in_sem, own_sem, out_sem, state_send, state_recv, halo_send, halo_recv,
+    gain, filt, lift, scanned, send, recv, kv_send, kv_recv, q_send, q_recv,
+    in_sem, own_sem, state_send, state_recv, halo_send, halo_recv,
 ):
     parts, tokens, width = held.shape
     margin = taps.shape[1] - 1
@@ -44,10 +44,6 @@
     def fetch(k):
         area = pl.ds(pl.multiple_of(k * span, span), span)
         return pltpu.make_async_copy(features.at[:, :, area], held.at[:, :, area], in_sem.at[k])
-
-    def put(k):
-        area = pl.ds(pl.multiple_of(k * span, span), span)
-        return pltpu.make_async_copy(result.at[:, area], out.at[:, area], out_sem.at[k])
 
     def state_copy(k):
         return pltpu.make_async_remote_copy(
@@ -245,16 +241,12 @@
 
     @pl.when(first)
     def _():
-        for i in range(margin):
-            row = history[i].astype(F32)
-            for j in range(parts):
-                for c in range(columns):
-                    ext[j, c, 8 - margin + i : 9 - margin + i] = row[
-                        j : j + 1, c * LANES : (c + 1) * LANES
-                    ]
-
         def begin(c, carry):
             recv[c // per_chunk, c % per_chunk] = start[:, lanes(c)]
+            for i in range(margin):
+                row = history[i, :, lanes(c)].astype(F32)
+                for j in range(parts):
+                    ext[j, c, 8 - margin + i : 9 - margin + i] = row[j : j + 1]
             return carry
 
         lax.fori_loop(0, columns, begin, 0)
@@ -352,7 +344,7 @@
                 terms = [terms[i] + terms[i + 1] for i in range(0, len(terms), 2)]
             value = query[c, t] * (inner[c, t] + terms[0])
             ext[0, c, pl.ds(t, SEG, stride=length), :] = value
-        result[:, lanes(c)] = ext[0, c, 0:tokens].astype(jnp.bfloat16)
+        out[:, lanes(c)] = ext[0, c, 0:tokens].astype(jnp.bfloat16)
         return carry
 
     def third_pass(k, carry):
@@ -361,7 +353,6 @@
             state_copy(k).wait_recv()
 
         each(k, correct)
-        put(k).start()
         return carry
 
     lax.fori_loop(0, chunks, third_pass, 0)
@@ -372,23 +363,6 @@
         q_copy.wait_send()
         for k in range(chunks):
             state_copy(k).wait_send()
-
-    for k in range(chunks):
-        put(k).wait()
-
-
-def settle(parts, source, out, sem):
-    rows = source.shape[0] // parts
-    copies = [
-        pltpu.make_async_copy(
-            source.at[pl.ds(i * rows, rows)], out.at[pl.ds(i * rows, rows)], sem.at[i]
-        )
-        for i in range(parts)
-    ]
-    for copy in copies:
-        copy.start()
-    for copy in copies:
-        copy.wait()
 
 
 def body(features, conv_weight, history, pole_rate, residue, skip_gain, start_state):
@@ -402,11 +376,11 @@
     hbm = pl.BlockSpec(memory_space=pltpu.HBM)
     small = pltpu.VMEM((columns, poles, LANES), F32)
     dma = pltpu.SemaphoreType.DMA
-    mixed = pl.pallas_call(
+    return pl.pallas_call(
         functools.partial(mixer, count, per_chunk),
-        out_shape=jax.ShapeDtypeStruct((tokens, width), jnp.bfloat16),
+        out_shape=pltpu.VMEM((tokens, width), jnp.bfloat16),
         in_specs=[hbm] * 7,
-        out_specs=hbm,
+        out_specs=pl.BlockSpec(memory_space=pltpu.VMEM),
         scratch_shapes=[
             pltpu.VMEM((parts,) + conv_weight.shape[:1] + (width,), jnp.bfloat16),
             pltpu.VMEM(history.shape, jnp.bfloat16),
@@ -431,8 +405,7 @@
             pltpu.VMEM((16, width), jnp.bfloat16),
             pltpu.VMEM((16, width // 2), jnp.bfloat16),
             pltpu.VMEM((16, width // 2), jnp.bfloat16),
-            pltpu.VMEM((tokens, width), jnp.bfloat16),
-            dma((chunks,)), dma((7,)), dma((chunks,)), dma((chunks,)), dma((chunks,)),
+            dma((chunks,)), dma((7,)), dma((chunks,)), dma((chunks,)),
             dma((2,)), dma((2,)),
         ],
         compiler_params=pltpu.CompilerParams(
@@ -442,14 +415,6 @@
         features.transpose(1, 0, 2), conv_weight.transpose(1, 0, 2), history,
         pole_rate, residue, skip_gain[None], start_state,
     )
-    pieces = tokens // 16
-    return pl.pallas_call(
-        functools.partial(settle, pieces),
-        out_shape=jax.ShapeDtypeStruct((tokens, width), jnp.bfloat16),
-        in_specs=[hbm],
-        out_specs=hbm,
-        scratch_shapes=[dma((pieces,))],
-    )(mixed)
 
 
 def solution(mesh):

time: 30.7 us -> 13.8 us (0.45)
  Pallas kernels: 30.6 us -> 12.8 us
  local copies, waits for them, and re-layouts: 0 us -> 0.8 us
    pallas_call x2 -> x1, Pallas kernels: 30.6 us -> 12.8 us  [body(): pl.pallas_call(functools.partial(mixer, count, per_chunk), out_shape=pltp...]
    unnamed x0 -> x1, local copies, waits for them, and re-layouts: none -> 0.8 us
where the time goes in v4:
time: 13.8 us; the launch traced here: 13.6 us
  Pallas kernels  12.8 us (93%)
  local copies, waits for them, and re-layouts  0.8 us (6%)
    pallas_call x1, Pallas kernels, body(): pl.pallas_call(functools.partial(mixer, count, per_chunk), out_shape=pltp...  12.8 us
    unnamed x1, local copies, waits for them, and re-layouts  0.8 us

profile of v4, /device:TPU:26, one launch (start us, length us, event | category | flops | bytes accessed | tf_op | source)
XLA Modules:
  0.0 13.6 jit_solution(3248698900602979714)
XLA Ops:
  0.0 12.8 %shard_map.73 = bf16[128,2048]{1,0:T(8,128)(2,1)S(1)} custom-call(bf16[3,128,2048]{2,1,0:T(8,128)(2,1)} %bitcast.3, bf16[3,7,2048]{2,1,0:T(8,128)(2,1)} %bitcast.4, bf16[6,3,2048]{2,1,0:T(4,128)(2,1)} %history_in.1, f32[16,2048]{1,0:T(8,128)} %rate_in.1, f32[16,2048]{1,0:T(8,128)} %residue_in.1, f32[1,2048]{1,0:T(1,128)} %bitcast.5, f32[16,2048]{1,0:T(8,128)} %start_in.1), custom_call_target="tpu_custom_call" | custom-call | tf_op jit(solution)/shard_map/pallas_call | solution.py:379
  12.8 0.8 %copy.9 = bf16[128,2048]{1,0:T(8,128)(2,1)} copy(bf16[128,2048]{1,0:T(8,128)(2,1)S(1)} %shard_map.73) | data formatting | bytes 1048576

commit v5 on v4

--- a/solution.py
+++ b/solution.py
@@ -154,13 +154,14 @@
 
     lax.fori_loop(0, columns // 2, pack_q, 0)
 
-    peers = jnp.where(first, 0, 1) + jnp.where(last, 0, 1)
-    pl.semaphore_wait(barrier, peers)
-
-    @pl.when(jnp.logical_not(last))
-    def _():
-        kv_copy.start()
-        q_copy.start()
+    def greet():
+        peers = jnp.where(first, 0, 1) + jnp.where(last, 0, 1)
+        pl.semaphore_wait(barrier, peers)
+
+        @pl.when(jnp.logical_not(last))
+        def _():
+            kv_copy.start()
+            q_copy.start()
 
     def filtered(j, c, low, high):
         x = [ext[j, c, pl.ds(8 + i, SEG, stride=length), :] for i in range(low - margin, high)]
@@ -256,6 +257,10 @@
             each(k, widen)
             each(k, end_states)
 
+            @pl.when(k == 0)
+            def _():
+                greet()
+
             @pl.when(jnp.logical_not(last))
             def _():
                 hand_on(k)
@@ -266,6 +271,8 @@
 
     @pl.when(jnp.logical_not(first))
     def _():
+        greet()
+
         def early_pass(k, carry):
             fetch(k).wait()
             each(k, widen)

time: 13.8 us -> 15.2 us (1.10)
  Pallas kernels: 12.8 us -> 14.2 us
    pallas_call x1, Pallas kernels: 12.8 us -> 14.2 us  [body(): pl.pallas_call(functools.partial(mixer, count, per_chunk), out_shape=pltp...]
where the time goes in v5:
time: 15.2 us; the launch traced here: 15.1 us
  Pallas kernels  14.2 us (93%)
  local copies, waits for them, and re-layouts  0.8 us (5%)
    pallas_call x1, Pallas kernels, body(): pl.pallas_call(functools.partial(mixer, count, per_chunk), out_shape=pltp...  14.2 us
    unnamed x1, local copies, waits for them, and re-layouts  0.8 us

profile of v5, /device:TPU:26, one launch (start us, length us, event | category | flops | bytes accessed | tf_op | source)
XLA Modules:
  0.0 15.1 jit_solution(487561841852396561)
XLA Ops:
  0.0 14.2 %shard_map.73 = bf16[128,2048]{1,0:T(8,128)(2,1)S(1)} custom-call(bf16[3,128,2048]{2,1,0:T(8,128)(2,1)} %bitcast.3, bf16[3,7,2048]{2,1,0:T(8,128)(2,1)} %bitcast.4, bf16[6,3,2048]{2,1,0:T(4,128)(2,1)} %history_in.1, f32[16,2048]{1,0:T(8,128)} %rate_in.1, f32[16,2048]{1,0:T(8,128)} %residue_in.1, f32[1,2048]{1,0:T(1,128)} %bitcast.5, f32[16,2048]{1,0:T(8,128)} %start_in.1), custom_call_target="tpu_custom_call" | custom-call | tf_op jit(solution)/shard_map/pallas_call | solution.py:386
  14.3 0.8 %copy.9 = bf16[128,2048]{1,0:T(8,128)(2,1)} copy(bf16[128,2048]{1,0:T(8,128)(2,1)S(1)} %shard_map.73) | data formatting | bytes 1048576

commit v6 on v4

--- a/solution.py
+++ b/solution.py
@@ -369,7 +369,7 @@
     tokens, parts, width = features.shape
     poles = pole_rate.shape[0]
     columns = width // LANES
-    per_chunk = 2
+    per_chunk = 1
     chunks = columns // per_chunk
     length = tokens // SEG
     count = lax.axis_size("seq")

time: 13.8 us -> 14 us (1.014)
  Pallas kernels: 12.8 us -> 13 us
    pallas_call x1, Pallas kernels: 12.8 us -> 13 us  [body(): pl.pallas_call(functools.partial(mixer, count, per_chunk), out_shape=pltp...]
where the time goes in v6:
time: 14 us; the launch traced here: 13.8 us
  Pallas kernels  13 us (93%)
  local copies, waits for them, and re-layouts  0.8 us (6%)
    pallas_call x1, Pallas kernels, body(): pl.pallas_call(functools.partial(mixer, count, per_chunk), out_shape=pltp...  13 us
    unnamed x1, local copies, waits for them, and re-layouts  0.8 us

profile of v6, /device:TPU:26, one launch (start us, length us, event | category | flops | bytes accessed | tf_op | source)
XLA Modules:
  0.0 13.8 jit_solution(13508738162985270382)
XLA Ops:
  0.0 13.0 %shard_map.73 = bf16[128,2048]{1,0:T(8,128)(2,1)S(1)} custom-call(bf16[3,128,2048]{2,1,0:T(8,128)(2,1)} %bitcast.3, bf16[3,7,2048]{2,1,0:T(8,128)(2,1)} %bitcast.4, bf16[6,3,2048]{2,1,0:T(4,128)(2,1)} %history_in.1, f32[16,2048]{1,0:T(8,128)} %rate_in.1, f32[16,2048]{1,0:T(8,128)} %residue_in.1, f32[1,2048]{1,0:T(1,128)} %bitcast.5, f32[16,2048]{1,0:T(8,128)} %start_in.1), custom_call_target="tpu_custom_call" | custom-call | tf_op jit(solution)/shard_map/pallas_call | solution.py:379
  13.0 0.8 %copy.9 = bf16[128,2048]{1,0:T(8,128)(2,1)} copy(bf16[128,2048]{1,0:T(8,128)(2,1)S(1)} %shard_map.73) | data formatting | bytes 1048576
